TPU v7x, 32 devices: a whole 2x2x4 slice. The times are simulated.
32 devices in a mesh: space: 8 (over y, x, core), lane: 4 (over z).
Axes of the slice: x: 2, y: 2, z: 4, core: 2. Of those that a mesh axis runs over, the one named last changes fastest.
Arguments:
- positions: float32 [256, 3, 544], P('space'), may hold values from -6 to 6
- bend_op: float32 [544, 544], replicated, may hold values from -0.25 to 0.25
- send_list: int32 [8, 8], P('space'), may hold values from 0 to 31
- task_target: int32 [32, 12], P(('space', 'lane')), may hold values from 0 to 31, as said below
- task_source: int32 [32, 12], P(('space', 'lane')), may hold values from 0 to 39, as said below
- task_count: int32 [32], P(('space', 'lane')), may hold values from 4 to 12, as said below
Outputs:
- moved_positions: float32 [256, 3, 544], P(('space', 'lane'))
- velocity: float32 [256, 3, 544], P(('space', 'lane'))
Inputs may be any that keep to these rules, and one draw needn't show every extreme that they name: `task_target`: slots at or beyond the list's task_count hold 0. `task_source`: slots at or beyond the list's task_count hold 0. Every received cell of an owner is the source of at least one live slot of that owner. `task_count`: in each owner exactly one lane has 12 live slots; every other lane has at most 7.
All inputs are finite; a program needn't handle non-finite values.
Results may differ from a plain program's by a relative error of at most 0.00015.
Values sent between devices are 32-bit elements; how exact they have to be, the bound alone decides.
No kernel may reach another device: no remote copies, remote signals or barrier semaphores. Data moves between devices by JAX's collectives and lax.ppermute only.
A program may use at most 64 MiB of HBM per device.

v0:
```python
import jax
import jax.numpy as jnp
from jax import lax
from jax.sharding import PartitionSpec as P

G = 1
TASK_CAP = 12
ITERS = 2


REGULARIZE = 0.25
TIME_STEP = 0.5


def stokes_tile(target_pos, source_pos, source_force):
    off_x = target_pos[0][:, None] - source_pos[0][None, :]
    off_y = target_pos[1][:, None] - source_pos[1][None, :]
    off_z = target_pos[2][:, None] - source_pos[2][None, :]
    distance_sq = off_x * off_x + off_y * off_y + off_z * off_z
    inverse = lax.rsqrt(distance_sq + REGULARIZE)
    inverse_cube = inverse * inverse * inverse
    projected = (
        off_x * source_force[0][None, :]
        + off_y * source_force[1][None, :]
        + off_z * source_force[2][None, :]
    )
    weight_direct = (distance_sq + 2.0 * REGULARIZE) * inverse_cube
    weight_tensor = projected * inverse_cube
    comp_x = jnp.sum(weight_direct * source_force[0][None, :] + weight_tensor * off_x, axis=1)
    comp_y = jnp.sum(weight_direct * source_force[1][None, :] + weight_tensor * off_y, axis=1)
    comp_z = jnp.sum(weight_direct * source_force[2][None, :] + weight_tensor * off_z, axis=1)
    return jnp.stack([comp_x, comp_y, comp_z], axis=0) / source_pos.shape[1]


def bending(current, bend_op):
    flattened = current.reshape(-1, current.shape[-1])
    return jnp.dot(
        flattened, bend_op, precision=lax.Precision.HIGHEST, preferred_element_type=jnp.float32
    ).reshape(current.shape)


def tile_batch(pool_pos, pool_frc, slot_targets, slot_sources, live_mask):
    target_rows = pool_pos[slot_targets]
    source_rows = pool_pos[slot_sources]
    force_rows = pool_frc[slot_sources]

    def single(bundle):
        return stokes_tile(bundle[0], bundle[1], bundle[2])

    tiles = lax.map(single, (target_rows, source_rows, force_rows))
    return tiles * live_mask.astype(jnp.float32)[:, None, None]


def shards(positions, bend_op, send_list, task_target, task_source, task_count):
    owners = lax.axis_size("space")
    lane_count = lax.axis_size("lane")
    lane_index = lax.axis_index("lane")
    cells_owner = positions.shape[0]
    points = positions.shape[2]
    share_rows = cells_owner // lane_count
    slot_targets = task_target[0]
    slot_sources = task_source[0]
    live_mask = jnp.arange(TASK_CAP, dtype=jnp.int32) < task_count[0]
    slot_targets = jnp.where(live_mask, slot_targets, 0)
    slot_sources = jnp.where(live_mask, slot_sources, 0)
    cell_ids = jnp.arange(cells_owner, dtype=jnp.int32)
    current = positions
    moved = positions[:share_rows]
    velocity = jnp.zeros_like(moved)
    for iteration in range(ITERS):
        forces = bending(current, bend_op)
        packed = jnp.concatenate([current, forces], axis=1).reshape(cells_owner, 6 * points)
        outgoing = packed[send_list[0]].reshape(owners, G, 6 * points)
        incoming = lax.all_to_all(outgoing, "space", split_axis=0, concat_axis=0, tiled=True)
        pool_rows = jnp.concatenate([packed, incoming.reshape(-1, 6 * points)], axis=0).reshape(
            -1, 2, 3, points
        )
        pool_pos = pool_rows[:, 0]
        pool_frc = pool_rows[:, 1]
        tiles = tile_batch(pool_pos, pool_frc, slot_targets, slot_sources, live_mask)
        tile_ids = jnp.where(live_mask, slot_targets, -1).astype(jnp.float32)
        all_rows, all_ids = (
            lax.all_gather(tiles, "lane", axis=0, tiled=True),
            lax.all_gather(tile_ids, "lane", axis=0, tiled=True),
        )
        every_match = (cell_ids.astype(jnp.float32)[:, None] == all_ids[None, :]).astype(
            jnp.float32
        )
        summed_speeds = jnp.dot(
            every_match,
            all_rows.reshape(-1, 3 * points),
            precision=lax.Precision.HIGHEST,
            preferred_element_type=jnp.float32,
        ).reshape(cells_owner, 3, points)
        current = current + TIME_STEP * summed_speeds
        velocity = lax.dynamic_slice_in_dim(summed_speeds, lane_index * share_rows, share_rows, 0)
        moved = lax.dynamic_slice_in_dim(current, lane_index * share_rows, share_rows, 0)
    return (moved, velocity)


def solution(mesh):
    in_specs = (
        P("space", None, None),
        P(),
        P("space", None),
        P(("space", "lane"), None),
        P(("space", "lane"), None),
        P(("space", "lane")),
    )
    out_specs = (P(("space", "lane"), None, None), P(("space", "lane"), None, None))
    return jax.shard_map(shards, mesh=mesh, in_specs=in_specs, out_specs=out_specs, check_vma=False)
```

profile of v0, /device:TPU:0, one launch (start us, length us, event | category | flops | bytes accessed | tf_op | source)
XLA Modules:
  0.0 133.3 jit_solution(11178519239515329744)
XLA Ops:
  6.1 5.2 %all-to-all-start = ((f32[8,1,3264]{2,1,0:T(1,128)}), f32[8,1,3264]{2,1,0:T(1,128)S(1)}, u32[]{:S(2)}, u32[]{:S(2)}) async-start(f32[8,1,3264]{2,1,0:T(1,128)} %copy.29), calls=%async_computation | async-start | bytes 212992 | tf_op jit(solution)/shard_map/all_to_all | solution.py:74
  13.8 11.9 %all-reduce = f32[48]{0:T(128)S(1)} all-reduce(f32[48]{0:T(128)S(1)} %fusion.49), channel_id=1, replica_groups=mesh['space'=8,'lane'=4] {'lane'}, use_global_device_ids=true, to_apply=%add | all-reduce | flops 48 | bytes 384
  28.3 27.8 %while.20 = (s32[]{:T(128)}, f32[12,3,544]{2,1,0:T(4,128)S(1)}, f32[12,3,544]{2,1,0:T(4,128)S(1)}, f32[12,3,544]{2,1,0:T(4,128)S(1)}, f32[12,3,544]{2,1,0:T(4,128)S(1)}, /*index=5*/s32[]{:T(128)}, s32[]{:T(128)}, s32[]{}, s32[]{}) while((s32[]{:T(128)}, f32[12,3,544]{2,1,0:T(4,128)S(1)}, f32[12,3,544]{2,1,0:T(4,128)S(1)}, ...), condition=%wide.region_4.5_spmd, body=%wide.region_0.4_spmd.sunk | while | flops 9177284 | bytes 96401 | solution.py:50
  28.4 2.1 %fusion.59 = (f32[544]{0:T(1024)S(1)}, f32[544]{0:T(1024)S(1)}, f32[544]{0:T(1024)S(1)}) fusion(f32[544]{0:T(1024)S(1)} %get-tuple-element.197, f32[544]{0:T(1024)S(1)} %get-tuple-element.198, f32[544]{0:T(1024)S(1)} %get-tuple-element.199, f32[544]{0:T(1024)S(1)} %get-tuple-element.200, f32[544]{0:T(1024)S(1)} %get-tuple-element.201, ...), kind=kLoop, calls=%fused_computation.24.clone.1 | loop fusion | flops 9172384 | bytes 26112 | tf_op jit(solution)/shard_map/while/body/eval_jaxpr/reduce_sum | solution.py:29
  30.7 2.1 %fusion.59 = (f32[544]{0:T(1024)S(1)}, f32[544]{0:T(1024)S(1)}, f32[544]{0:T(1024)S(1)}) fusion(f32[544]{0:T(1024)S(1)} %get-tuple-element.197, f32[544]{0:T(1024)S(1)} %get-tuple-element.198, f32[544]{0:T(1024)S(1)} %get-tuple-element.199, f32[544]{0:T(1024)S(1)} %get-tuple-element.200, f32[544]{0:T(1024)S(1)} %get-tuple-element.201, ...), kind=kLoop, calls=%fused_computation.24.clone.1 | loop fusion | flops 9172384 | bytes 26112 | tf_op jit(solution)/shard_map/while/body/eval_jaxpr/reduce_sum | solution.py:29
  42.3 2.1 %fusion.59 = (f32[544]{0:T(1024)S(1)}, f32[544]{0:T(1024)S(1)}, f32[544]{0:T(1024)S(1)}) fusion(f32[544]{0:T(1024)S(1)} %get-tuple-element.197, f32[544]{0:T(1024)S(1)} %get-tuple-element.198, f32[544]{0:T(1024)S(1)} %get-tuple-element.199, f32[544]{0:T(1024)S(1)} %get-tuple-element.200, f32[544]{0:T(1024)S(1)} %get-tuple-element.201, ...), kind=kLoop, calls=%fused_computation.24.clone.1 | loop fusion | flops 9172384 | bytes 26112 | tf_op jit(solution)/shard_map/while/body/eval_jaxpr/reduce_sum | solution.py:29
  44.6 2.1 %fusion.59 = (f32[544]{0:T(1024)S(1)}, f32[544]{0:T(1024)S(1)}, f32[544]{0:T(1024)S(1)}) fusion(f32[544]{0:T(1024)S(1)} %get-tuple-element.197, f32[544]{0:T(1024)S(1)} %get-tuple-element.198, f32[544]{0:T(1024)S(1)} %get-tuple-element.199, f32[544]{0:T(1024)S(1)} %get-tuple-element.200, f32[544]{0:T(1024)S(1)} %get-tuple-element.201, ...), kind=kLoop, calls=%fused_computation.24.clone.1 | loop fusion | flops 9172384 | bytes 26112 | tf_op jit(solution)/shard_map/while/body/eval_jaxpr/reduce_sum | solution.py:29
  56.1 14.8 %all_gather.11 = f32[48,3,544]{2,1,0:T(4,128)S(1)} all-gather(f32[12,3,544]{2,1,0:T(4,128)S(1)} %broadcast_multiply_fusion.1), channel_id=1, replica_groups=mesh['space'=8,'lane'=4] {'lane'}, dimensions={0}, use_global_device_ids=true | all-gather | bytes 391680 | tf_op jit(solution)/shard_map/all_gather | solution.py:83
  74.7 4.0 %all-to-all-start.1 = ((f32[8,1,3264]{2,1,0:T(1,128)}), f32[8,1,3264]{2,1,0:T(1,128)S(1)}, u32[]{:S(2)}, u32[]{:S(2)}) async-start(f32[8,1,3264]{2,1,0:T(1,128)} %copy.34), calls=%async_computation.1 | async-start | bytes 212992 | tf_op jit(solution)/shard_map/all_to_all | solution.py:74
  79.1 4.9 %all-to-all-done.1 = f32[8,1,3264]{2,1,0:T(1,128)S(1)} async-done(((f32[8,1,3264]{2,1,0:T(1,128)}), f32[8,1,3264]{2,1,0:T(1,128)S(1)}, u32[]{:S(2)}, u32[]{:S(2)}) %all-to-all-start.1) | async-done | bytes 104480 | tf_op jit(solution)/shard_map/all_to_all | solution.py:74
  88.2 27.8 %while.21 = (s32[]{:T(128)}, f32[12,3,544]{2,1,0:T(4,128)S(1)}, f32[12,3,544]{2,1,0:T(4,128)S(1)}, f32[12,3,544]{2,1,0:T(4,128)S(1)}, f32[12,3,544]{2,1,0:T(4,128)S(1)}, /*index=5*/s32[]{:T(128)}, s32[]{:T(128)}, s32[]{}, s32[]{}) while((s32[]{:T(128)}, f32[12,3,544]{2,1,0:T(4,128)S(1)}, f32[12,3,544]{2,1,0:T(4,128)S(1)}, ...), condition=%wide.region_9.10_spmd, body=%wide.region_5.9_spmd.sunk | while | flops 9177284 | bytes 96401 | solution.py:50
  88.4 2.1 %fusion.61 = (f32[544]{0:T(1024)S(1)}, f32[544]{0:T(1024)S(1)}, f32[544]{0:T(1024)S(1)}) fusion(f32[544]{0:T(1024)S(1)} %get-tuple-element.214, f32[544]{0:T(1024)S(1)} %get-tuple-element.215, f32[544]{0:T(1024)S(1)} %get-tuple-element.216, f32[544]{0:T(1024)S(1)} %get-tuple-element.217, f32[544]{0:T(1024)S(1)} %get-tuple-element.218, ...), kind=kLoop, calls=%fused_computation.60.clone.1 | loop fusion | flops 9172384 | bytes 26112 | tf_op jit(solution)/shard_map/while/body/eval_jaxpr/reduce_sum | solution.py:29
  90.7 2.1 %fusion.61 = (f32[544]{0:T(1024)S(1)}, f32[544]{0:T(1024)S(1)}, f32[544]{0:T(1024)S(1)}) fusion(f32[544]{0:T(1024)S(1)} %get-tuple-element.214, f32[544]{0:T(1024)S(1)} %get-tuple-element.215, f32[544]{0:T(1024)S(1)} %get-tuple-element.216, f32[544]{0:T(1024)S(1)} %get-tuple-element.217, f32[544]{0:T(1024)S(1)} %get-tuple-element.218, ...), kind=kLoop, calls=%fused_computation.60.clone.1 | loop fusion | flops 9172384 | bytes 26112 | tf_op jit(solution)/shard_map/while/body/eval_jaxpr/reduce_sum | solution.py:29
  93.0 2.1 %fusion.61 = (f32[544]{0:T(1024)S(1)}, f32[544]{0:T(1024)S(1)}, f32[544]{0:T(1024)S(1)}) fusion(f32[544]{0:T(1024)S(1)} %get-tuple-element.214, f32[544]{0:T(1024)S(1)} %get-tuple-element.215, f32[544]{0:T(1024)S(1)} %get-tuple-element.216, f32[544]{0:T(1024)S(1)} %get-tuple-element.217, f32[544]{0:T(1024)S(1)} %get-tuple-element.218, ...), kind=kLoop, calls=%fused_computation.60.clone.1 | loop fusion | flops 9172384 | bytes 26112 | tf_op jit(solution)/shard_map/while/body/eval_jaxpr/reduce_sum | solution.py:29
  95.3 2.1 %fusion.61 = (f32[544]{0:T(1024)S(1)}, f32[544]{0:T(1024)S(1)}, f32[544]{0:T(1024)S(1)}) fusion(f32[544]{0:T(1024)S(1)} %get-tuple-element.214, f32[544]{0:T(1024)S(1)} %get-tuple-element.215, f32[544]{0:T(1024)S(1)} %get-tuple-element.216, f32[544]{0:T(1024)S(1)} %get-tuple-element.217, f32[544]{0:T(1024)S(1)} %get-tuple-element.218, ...), kind=kLoop, calls=%fused_computation.60.clone.1 | loop fusion | flops 9172384 | bytes 26112 | tf_op jit(solution)/shard_map/while/body/eval_jaxpr/reduce_sum | solution.py:29
  97.6 2.1 %fusion.61 = (f32[544]{0:T(1024)S(1)}, f32[544]{0:T(1024)S(1)}, f32[544]{0:T(1024)S(1)}) fusion(f32[544]{0:T(1024)S(1)} %get-tuple-element.214, f32[544]{0:T(1024)S(1)} %get-tuple-element.215, f32[544]{0:T(1024)S(1)} %get-tuple-element.216, f32[544]{0:T(1024)S(1)} %get-tuple-element.217, f32[544]{0:T(1024)S(1)} %get-tuple-element.218, ...), kind=kLoop, calls=%fused_computation.60.clone.1 | loop fusion | flops 9172384 | bytes 26112 | tf_op jit(solution)/shard_map/while/body/eval_jaxpr/reduce_sum | solution.py:29
  99.9 2.1 %fusion.61 = (f32[544]{0:T(1024)S(1)}, f32[544]{0:T(1024)S(1)}, f32[544]{0:T(1024)S(1)}) fusion(f32[544]{0:T(1024)S(1)} %get-tuple-element.214, f32[544]{0:T(1024)S(1)} %get-tuple-element.215, f32[544]{0:T(1024)S(1)} %get-tuple-element.216, f32[544]{0:T(1024)S(1)} %get-tuple-element.217, f32[544]{0:T(1024)S(1)} %get-tuple-element.218, ...), kind=kLoop, calls=%fused_computation.60.clone.1 | loop fusion | flops 9172384 | bytes 26112 | tf_op jit(solution)/shard_map/while/body/eval_jaxpr/reduce_sum | solution.py:29
  102.3 2.1 %fusion.61 = (f32[544]{0:T(1024)S(1)}, f32[544]{0:T(1024)S(1)}, f32[544]{0:T(1024)S(1)}) fusion(f32[544]{0:T(1024)S(1)} %get-tuple-element.214, f32[544]{0:T(1024)S(1)} %get-tuple-element.215, f32[544]{0:T(1024)S(1)} %get-tuple-element.216, f32[544]{0:T(1024)S(1)} %get-tuple-element.217, f32[544]{0:T(1024)S(1)} %get-tuple-element.218, ...), kind=kLoop, calls=%fused_computation.60.clone.1 | loop fusion | flops 9172384 | bytes 26112 | tf_op jit(solution)/shard_map/while/body/eval_jaxpr/reduce_sum | solution.py:29
  104.6 2.1 %fusion.61 = (f32[544]{0:T(1024)S(1)}, f32[544]{0:T(1024)S(1)}, f32[544]{0:T(1024)S(1)}) fusion(f32[544]{0:T(1024)S(1)} %get-tuple-element.214, f32[544]{0:T(1024)S(1)} %get-tuple-element.215, f32[544]{0:T(1024)S(1)} %get-tuple-element.216, f32[544]{0:T(1024)S(1)} %get-tuple-element.217, f32[544]{0:T(1024)S(1)} %get-tuple-element.218, ...), kind=kLoop, calls=%fused_computation.60.clone.1 | loop fusion | flops 9172384 | bytes 26112 | tf_op jit(solution)/shard_map/while/body/eval_jaxpr/reduce_sum | solution.py:29
  106.9 2.1 %fusion.61 = (f32[544]{0:T(1024)S(1)}, f32[544]{0:T(1024)S(1)}, f32[544]{0:T(1024)S(1)}) fusion(f32[544]{0:T(1024)S(1)} %get-tuple-element.214, f32[544]{0:T(1024)S(1)} %get-tuple-element.215, f32[544]{0:T(1024)S(1)} %get-tuple-element.216, f32[544]{0:T(1024)S(1)} %get-tuple-element.217, f32[544]{0:T(1024)S(1)} %get-tuple-element.218, ...), kind=kLoop, calls=%fused_computation.60.clone.1 | loop fusion | flops 9172384 | bytes 26112 | tf_op jit(solution)/shard_map/while/body/eval_jaxpr/reduce_sum | solution.py:29
  109.2 2.1 %fusion.61 = (f32[544]{0:T(1024)S(1)}, f32[544]{0:T(1024)S(1)}, f32[544]{0:T(1024)S(1)}) fusion(f32[544]{0:T(1024)S(1)} %get-tuple-element.214, f32[544]{0:T(1024)S(1)} %get-tuple-element.215, f32[544]{0:T(1024)S(1)} %get-tuple-element.216, f32[544]{0:T(1024)S(1)} %get-tuple-element.217, f32[544]{0:T(1024)S(1)} %get-tuple-element.218, ...), kind=kLoop, calls=%fused_computation.60.clone.1 | loop fusion | flops 9172384 | bytes 26112 | tf_op jit(solution)/shard_map/while/body/eval_jaxpr/reduce_sum | solution.py:29
  111.5 2.1 %fusion.61 = (f32[544]{0:T(1024)S(1)}, f32[544]{0:T(1024)S(1)}, f32[544]{0:T(1024)S(1)}) fusion(f32[544]{0:T(1024)S(1)} %get-tuple-element.214, f32[544]{0:T(1024)S(1)} %get-tuple-element.215, f32[544]{0:T(1024)S(1)} %get-tuple-element.216, f32[544]{0:T(1024)S(1)} %get-tuple-element.217, f32[544]{0:T(1024)S(1)} %get-tuple-element.218, ...), kind=kLoop, calls=%fused_computation.60.clone.1 | loop fusion | flops 9172384 | bytes 26112 | tf_op jit(solution)/shard_map/while/body/eval_jaxpr/reduce_sum | solution.py:29
  113.8 2.1 %fusion.61 = (f32[544]{0:T(1024)S(1)}, f32[544]{0:T(1024)S(1)}, f32[544]{0:T(1024)S(1)}) fusion(f32[544]{0:T(1024)S(1)} %get-tuple-element.214, f32[544]{0:T(1024)S(1)} %get-tuple-element.215, f32[544]{0:T(1024)S(1)} %get-tuple-element.216, f32[544]{0:T(1024)S(1)} %get-tuple-element.217, f32[544]{0:T(1024)S(1)} %get-tuple-element.218, ...), kind=kLoop, calls=%fused_computation.60.clone.1 | loop fusion | flops 9172384 | bytes 26112 | tf_op jit(solution)/shard_map/while/body/eval_jaxpr/reduce_sum | solution.py:29
  116.1 15.7 %all_gather.12 = f32[48,3,544]{2,1,0:T(4,128)S(1)} all-gather(f32[12,3,544]{2,1,0:T(4,128)S(1)} %broadcast_multiply_fusion), channel_id=1, replica_groups=mesh['space'=8,'lane'=4] {'lane'}, dimensions={0}, use_global_device_ids=true | all-gather | bytes 391680 | tf_op jit(solution)/shard_map/all_gather | solution.py:83
  (214 shorter events, 39.0 us)
Async XLA Ops:
  0.6 1.4 %copy-start = (f32[544,544]{1,0:T(8,128)S(1)}, f32[544,544]{1,0:T(8,128)}, u32[]{:S(2)}) copy-start(f32[544,544]{1,0:T(8,128)} %param.11) | copy-start | bytes 3551236
  0.6 3.4 %copy-start.1 = (f32[32,3,544]{2,0,1:T(8,128)S(1)}, f32[32,3,544]{2,0,1:T(8,128)}, u32[]{:S(2)}) copy-start(f32[32,3,544]{2,0,1:T(8,128)} %param.10) | copy-start | bytes 626692
  4.0 0.7 copy-start.4
  4.4 7.5 %copy-start.2 = (s32[1,12]{1,0:T(1,128)S(1)}, s32[1,12]{1,0:T(1,128)}, u32[]{:S(2)}) copy-start(s32[1,12]{1,0:T(1,128)} %param.13) | copy-start | bytes 148
  4.4 7.5 %copy-start.3 = (s32[1,12]{1,0:T(1,128)S(1)}, s32[1,12]{1,0:T(1,128)}, u32[]{:S(2)}) copy-start(s32[1,12]{1,0:T(1,128)} %param.14) | copy-start | bytes 148
  4.7 7.6 %copy-start.5 = (u32[32]{0:T(128)S(1)}, u32[32]{0:T(128)}, u32[]{:S(2)}) copy-start(u32[32]{0:T(128)} %constant.65) | copy-start | bytes 388
  6.1 19.7 %all-to-all-start = ((f32[8,1,3264]{2,1,0:T(1,128)}), f32[8,1,3264]{2,1,0:T(1,128)S(1)}, u32[]{:S(2)}, u32[]{:S(2)}) async-start(f32[8,1,3264]{2,1,0:T(1,128)} %copy.29), calls=%async_computation | async-start | bytes 212992 | tf_op jit(solution)/shard_map/all_to_all | solution.py:74
  74.7 9.2 %all-to-all-start.1 = ((f32[8,1,3264]{2,1,0:T(1,128)}), f32[8,1,3264]{2,1,0:T(1,128)S(1)}, u32[]{:S(2)}, u32[]{:S(2)}) async-start(f32[8,1,3264]{2,1,0:T(1,128)} %copy.34), calls=%async_computation.1 | async-start | bytes 212992 | tf_op jit(solution)/shard_map/all_to_all | solution.py:74
where the time goes:
time: 134 us; the launch traced here: 133 us
  other arithmetic  53.3 us (40%)
  blocking collectives  42.4 us (32%)
  local copies, waits for them, and re-layouts  16 us (12%)
  starting transfers between devices  9.14 us (7%)
  waiting for transfers between devices  4.93 us (4%)
  matrix products  3.75 us (3%)
  between operations  2.35 us (2%)
  loops' own time  1.4 us (1%)
    reduce_sum x24, other arithmetic, stokes_tile(): jnp.sum(weight_direct * source_force[0][None, :] + weight_tensor * off_x,...  51.1 us
    all_gather x2, blocking collectives, shards(): lax.all_gather(tiles, 'lane', axis=0, tiled=True)  30.5 us
    unnamed x1, blocking collectives  11.9 us
    all_to_all x2, starting transfers between devices, shards(): lax.all_to_all(outgoing, 'space', split_axis=0, concat_axis=0, tiled=True)  9.14 us
    all_to_all x2, waiting for transfers between devices, shards(): lax.all_to_all(outgoing, 'space', split_axis=0, concat_axis=0, tiled=True)  4.93 us
    dot_general x2, matrix products, bending(): jnp.dot(flattened, bend_op, precision=lax.Precision.HIGHEST, preferred_el...  3.14 us
    unnamed x16, local copies, waits for them, and re-layouts  2.81 us
  transfers between devices with their start and end apart: 2, of which 1 were waited for; matrix products, arithmetic and copies ran while one was open for 1% of the time, Pallas kernels for 0%

commit v1 on v0

v1 whole, which is shorter than its diff:
```python
import functools
from types import SimpleNamespace

import jax
import jax.numpy as jnp
from jax import lax
from jax.experimental import pallas as pl
from jax.experimental.pallas import tpu as pltpu
from jax.sharding import PartitionSpec as P

REGULARIZE = 0.25
TIME_STEP = 0.5
UNROLL = 3
SOURCE_ROWS = 24
SUM_ROWS = 16

F32 = jnp.float32
BF16 = jnp.bfloat16
VMEM = pl.BlockSpec(memory_space=pltpu.VMEM)
SMEM = pl.BlockSpec(memory_space=pltpu.SMEM)
ANY = pl.BlockSpec(memory_space=pl.ANY)


def up(value, step):
    return -(-value // step) * step


def sizes(owners, lanes, cells, points, cap, listed):
    main = 128 * (points // (128 * lanes))
    rest = (points - main * lanes) // lanes
    group = listed // owners
    pool = up(cells + (owners - 1) * group, 8)
    per_pack = 128 // rest
    return SimpleNamespace(
        owners=owners,
        lanes=lanes,
        cells=cells,
        points=points,
        cap=cap,
        group=group,
        width=up(points, 128),
        tiles=up(points, 128) // 128,
        main=main,
        rest=rest,
        rest_tiles=up(rest * lanes, 128) // 128,
        chunk=main + rest,
        chunk_wide=main + up(rest, 128),
        chunk_tiles=(main + up(rest, 128)) // 128,
        per_pack=per_pack,
        pool=pool,
        share=cells // lanes,
        slots=up(lanes * cap + UNROLL, 8),
        rows=cells + 8,
    )


def pack_rows(sz, rows):
    return (3 * rows * sz.main // 128) + 8 * up(3 * rows // 8, sz.per_pack) // sz.per_pack


def split2(value):
    high = value.astype(BF16)
    return high, (value - high.astype(F32)).astype(BF16)


def split3(value):
    first = value.astype(BF16).astype(F32)
    left = value - first
    second = left.astype(BF16).astype(F32)
    return first, second, left - second


def lane_iota(rows):
    return lax.broadcasted_iota(jnp.int32, (rows, 128), 1)


def gather_kernel(sz, send, target, source, count, positions, *rest):
    outs, task_list, sems = rest[: sz.owners - 1], rest[sz.owners - 1], rest[sz.owners]
    me = lax.axis_index("space")
    copies = []
    for k in range(1, sz.owners):
        for g in range(sz.group):
            cell = send[0, (me ^ k) * sz.group + g]
            copies.append(
                pltpu.make_async_copy(
                    positions.at[pl.ds(cell, 1)], outs[k - 1].at[pl.ds(g, 1)], sems.at[k - 1, g]
                )
            )
    for copy in copies:
        copy.start()
    for j in range(sz.cap):
        task_list[0, j] = target[0, j]
        task_list[0, sz.cap + j] = source[0, j]
    task_list[0, 2 * sz.cap] = count[0]
    for copy in copies:
        copy.wait()


def build_list(sz, me, lists, send, tasks):
    total = jnp.int32(0)
    for one in lists:

        def step(j, total, one=one):
            source = one[0, sz.cap + j]
            ghost = jnp.maximum(source - sz.cells, 0)
            owner = lax.div(ghost, jnp.int32(sz.group))
            slot = sz.cells + ((owner ^ me) - 1) * sz.group + ghost - owner * sz.group
            received = jnp.where(owner == me, send[0, ghost], slot)
            tasks[0, total] = one[0, j]
            tasks[1, total] = jnp.where(source < sz.cells, source, received)
            return total + 1

        total = lax.fori_loop(0, one[0, 2 * sz.cap], step, total)
    for u in range(UNROLL):
        tasks[0, total + u] = jnp.int32(sz.cells)
        tasks[1, total + u] = jnp.int32(0)
    return total


def own_chunk(sz, lane, pool, first, rows):
    parts = []
    if sz.main:
        parts.append(pool[pl.ds(first, rows), pl.ds(pl.multiple_of(lane * sz.main, 128), sz.main)])
    start = sz.rest * lane
    lanes = lane_iota(rows)
    rest = jnp.zeros((rows, 128), F32)
    for tile in range(sz.rest_tiles):
        offset = sz.main * sz.lanes + 128 * tile
        block = pool[pl.ds(first, rows), offset : offset + 128]
        inside = (lanes + 128 * tile >= start) & (lanes + 128 * tile < start + sz.rest)
        rest = rest + jnp.where(inside, block, 0.0)
    rest = pltpu.roll(rest, lax.rem(128 * sz.rest_tiles - start, 128), 1)
    parts.append(rest)
    return jnp.concatenate(parts, axis=1) if len(parts) > 1 else parts[0]


def prepare(sz, lane, pool, bend, source_rows, centres, targets):
    value = pool[...]
    high, low = split2(value[:, : sz.points])
    bend_high, bend_low = split2(bend[...])
    dot = functools.partial(jnp.dot, preferred_element_type=F32)
    forces = dot(high, bend_high) + dot(low, bend_high) + dot(high, bend_low)
    forces = jnp.concatenate(
        [forces, jnp.zeros((3 * sz.pool, sz.width - sz.points), F32)], axis=1
    )
    middle = jnp.sum(value, axis=1, keepdims=True) / sz.points
    centres[...] = jnp.zeros_like(centres)
    for g in range(sz.pool // 8):
        where = [i * sz.pool + 8 * g for i in range(3)]
        middles = [jnp.broadcast_to(middle[w : w + 8], (8, 128)) for w in where]
        for i in range(3):
            centres[pl.ds(64 * g + i, 8, stride=8), :] = middles[i]
        for j in range(sz.tiles):
            cut = slice(128 * j, 128 * j + 128)
            y = [value[w : w + 8, cut] - m for w, m in zip(where, middles)]
            f = [forces[w : w + 8, cut] for w in where]
            norm = y[0] * y[0] + y[1] * y[1] + y[2] * y[2] + REGULARIZE
            along = y[0] * f[0] + y[1] * f[1] + y[2] * f[2]
            one, zero = jnp.ones((8, 128), F32), jnp.zeros((8, 128), F32)
            rows = [y[0], y[1], y[2], norm, one, zero, zero, zero]
            rows += f
            rows += [y[i] * f[k] for i in range(3) for k in range(3)]
            rows += [norm * f[i] + along * y[i] for i in range(3)]
            rows += [along]
            for k, row in enumerate(rows):
                source_rows.at[j][pl.ds(8 * SOURCE_ROWS * g + k, 8, stride=SOURCE_ROWS), :] = row
    targets[...] = jnp.zeros_like(targets)
    for g in range(sz.cells // 8):
        for i in range(3):
            chunk = own_chunk(sz, lane, pool, i * sz.pool + 8 * g, 8)
            for j in range(sz.chunk_tiles):
                targets.at[j][pl.ds(64 * g + i, 8, stride=8), :] = chunk[:, 128 * j : 128 * j + 128]


def one_task(sz, slot, tasks, source_rows, centres, targets, offsets, sums):
    target, source = tasks[0, slot], tasks[1, slot]
    centre = centres[pl.ds(pl.multiple_of(8 * source, 8), 8), :]
    row = lax.broadcasted_iota(jnp.int32, (8, 128), 0)
    pieces = []
    for j in range(sz.chunk_tiles):
        x = targets[j, pl.ds(pl.multiple_of(8 * target, 8), 8), :] - centre
        offsets.at[j][pl.ds(slot, 8, stride=sz.slots), :] = x
        square = x * x
        norm = pltpu.roll(square, 2, 0) + pltpu.roll(square, 3, 0) + pltpu.roll(square, 4, 0)
        side = jnp.where(row == 4, norm, jnp.where(row == 3, 1.0, 0.0))
        pieces.append(jnp.where(row < 3, -2.0 * x, side))
    x_side = jnp.concatenate(pieces, axis=1) if len(pieces) > 1 else pieces[0]
    x1, x2, x3 = split3(x_side)
    x_stack = jnp.concatenate([x1, x2, x1, x2, x3, x1], axis=0).astype(BF16)[:, : sz.chunk]
    held = jnp.concatenate(
        [
            source_rows[j, pl.ds(pl.multiple_of(SOURCE_ROWS * source, 8), SOURCE_ROWS), :]
            for j in range(sz.tiles)
        ],
        axis=1,
    )
    y1, y2, y3 = split3(held[:8])
    y_stack = jnp.concatenate([y1, y1, y2, y2, y1, y3], axis=0).astype(BF16)
    shifted = lax.dot_general(
        x_stack, y_stack, (((0,), (0,)), ((), ())), preferred_element_type=F32
    )
    inverse = lax.rsqrt(shifted)
    high, low = split2(inverse * inverse * inverse)
    m_stack = jnp.concatenate(split3(held[8:]), axis=0).astype(BF16)
    turned = (((1,), (1,)), ((), ()))
    result = lax.dot_general(m_stack, high, turned, preferred_element_type=F32)
    result = result + lax.dot_general(m_stack, low, turned, preferred_element_type=F32)
    result = result[:SUM_ROWS] + result[SUM_ROWS : 2 * SUM_ROWS] + result[2 * SUM_ROWS :]
    spare = sz.chunk_wide - sz.chunk
    if spare:
        result = jnp.concatenate([result, jnp.zeros((SUM_ROWS, spare), F32)], axis=1)
    for j in range(sz.chunk_tiles):
        for h in range(0, SUM_ROWS, 8):
            sums.at[j][pl.ds(h * sz.slots + slot, 8, stride=sz.slots), :] = result[
                h : h + 8, 128 * j : 128 * j + 128
            ]


def combine(sz, first, offsets, sums, speeds):
    for j in range(sz.chunk_tiles):
        x = [offsets[j, pl.ds(i * sz.slots + first, 8), :] for i in range(3)]
        s = [sums[j, pl.ds(k * sz.slots + first, 8), :] for k in range(SUM_ROWS)]
        a, b, c = s[:3], [s[3:6], s[6:9], s[9:12]], s[12:15]
        norm = x[0] * x[0] + x[1] * x[1] + x[2] * x[2] + REGULARIZE
        along = x[0] * a[0] + x[1] * a[1] + x[2] * a[2] - s[15]
        for i in range(3):
            speed = norm * a[i] + c[i] + along * x[i]
            for k in range(3):
                speed = speed - x[k] * (2.0 * b[k][i] + b[i][k])
            speeds[i, pl.ds(first, 8), 128 * j : 128 * j + 128] = speed / sz.points


def all_tiles(sz, total, tasks, source_rows, centres, targets, offsets, sums, speeds, moved):
    def several(q, carry):
        for u in range(UNROLL):
            one_task(sz, q * UNROLL + u, tasks, source_rows, centres, targets, offsets, sums)
        return carry

    lax.fori_loop(0, lax.div(total + UNROLL - 1, UNROLL), several, 0)

    def eight(q, carry):
        combine(sz, pl.multiple_of(8 * q, 8), offsets, sums, speeds)
        return carry

    lax.fori_loop(0, lax.div(total + 7, 8), eight, 0)
    moved[...] = jnp.zeros_like(moved)

    def add(t, carry):
        for i in range(3):
            place = pl.ds(i * sz.rows + tasks[0, t], 1)
            moved[place, :] = moved[place, :] + speeds[i, pl.ds(t, 1), :]
        return carry

    lax.fori_loop(0, total, add, 0)


def packed(sz, blocks):
    rows = [b[:, : sz.main] for b in blocks] if sz.main else []
    lanes = lane_iota(8)
    for p in range(0, len(blocks), sz.per_pack):
        total = jnp.zeros((8, 128), F32)
        for q, block in enumerate(blocks[p : p + sz.per_pack]):
            rest = jnp.where(lanes < sz.rest, block[:, sz.main : sz.main + 128], 0.0)
            total = total + (pltpu.roll(rest, q * sz.rest, 1) if q else rest)
        rows.append(total)
    return rows


def store_packed(sz, out, blocks):
    first = 0
    count = len(blocks)
    values = packed(sz, blocks)
    if sz.main:
        for b in range(count):
            for m in range(sz.main // 128):
                out[pl.ds(first, 8), :] = values[b][:, 128 * m : 128 * m + 128]
                first += 8
        values = values[count:]
    for value in values:
        out[pl.ds(first, 8), :] = value
        first += 8


def place_packed(sz, lane, arrived, count, store_main, add_rest):
    first = 0
    if sz.main:
        for b in range(count):
            for m in range(sz.main // 128):
                store_main(b, m, arrived[pl.ds(first, 8), :])
                first += 8
    start = sz.rest * lane
    lanes = lane_iota(8)
    for b in range(count):
        pack, q = divmod(b, sz.per_pack)
        value = arrived[pl.ds(first + 8 * pack, 8), :]
        value = pltpu.roll(value, lax.rem(start - q * sz.rest + 128, 128), 1)
        for tile in range(sz.rest_tiles):
            inside = (lanes + 128 * tile >= start) & (lanes + 128 * tile < start + sz.rest)
            add_rest(b, tile, jnp.where(inside, value, 0.0))


def first_kernel(sz, send, *refs):
    lists, refs = refs[: sz.lanes], refs[sz.lanes :]
    positions, refs = refs[0], refs[1:]
    ghosts, refs = refs[: sz.owners - 1], refs[sz.owners - 1 :]
    bend, chunk_out = refs[0], refs[1]
    ghost_out, refs = refs[2 : 1 + sz.owners], refs[1 + sz.owners :]
    pool, source_rows, centres, targets, offsets, sums, speeds, moved, tasks = refs
    me, lane = lax.axis_index("space"), lax.axis_index("lane")
    pool[...] = jnp.zeros_like(pool)
    for i in range(3):
        pool[pl.ds(i * sz.pool, sz.cells), : sz.points] = positions[:, i, :]
        for k in range(sz.owners - 1):
            for g in range(sz.group):
                place = i * sz.pool + sz.cells + k * sz.group + g
                pool[pl.ds(place, 1), : sz.points] = ghosts[k][g, pl.ds(i, 1), :]
    total = build_list(sz, me, lists, send, tasks)
    prepare(sz, lane, pool, bend, source_rows, centres, targets)
    all_tiles(sz, total, tasks, source_rows, centres, targets, offsets, sums, speeds, moved)
    blocks = []
    for i in range(3):
        for g in range(0, sz.cells, 8):
            chunk = own_chunk(sz, lane, pool, i * sz.pool + g, 8)
            place = pl.ds(i * sz.rows + g, 8)
            block = chunk + TIME_STEP * moved[place, :]
            moved[place, :] = block
            blocks.append(block)
    store_packed(sz, chunk_out, blocks)
    lanes = lane_iota(1)
    for k in range(1, sz.owners):
        for g in range(sz.group):
            cell = send[0, (me ^ k) * sz.group + g]
            rest = jnp.zeros((1, 128), F32)
            for i in range(3):
                place = pl.ds(i * sz.rows + cell, 1)
                row = moved[place, :]
                if sz.main:
                    ghost_out[k - 1][pl.ds(4 * g + i, 1), :] = row[:, :128]
                else:
                    ghost_out[k - 1][pl.ds(4 * g + i, 1), :] = jnp.zeros((1, 128), F32)
                piece = jnp.where(lanes < sz.rest, row[:, sz.main : sz.main + 128], 0.0)
                rest = rest + (pltpu.roll(piece, i * sz.rest, 1) if i else piece)
            ghost_out[k - 1][pl.ds(4 * g + 3, 1), :] = rest


def second_kernel(sz, send, *refs):
    lists, refs = refs[: sz.lanes], refs[sz.lanes :]
    chunks, refs = refs[: sz.lanes], refs[sz.lanes :]
    ghosts, refs = refs[: sz.lanes], refs[sz.lanes :]
    bend = refs[0]
    outs, refs = refs[1 : 1 + sz.lanes], refs[1 + sz.lanes :]
    share_out = refs[0]
    pool, source_rows, centres, targets, offsets, sums, speeds, moved, tasks = refs[1:]
    me, lane = lax.axis_index("space"), lax.axis_index("lane")
    pool[...] = jnp.zeros_like(pool)
    per = sz.cells // 8
    for k in range(sz.lanes):
        other = lane ^ k

        def row_of(b):
            return (b // per) * sz.pool + 8 * (b % per)

        def store_main(b, m, value):
            cut = pl.ds(pl.multiple_of(other * sz.main + 128 * m, 128), 128)
            pool[pl.ds(row_of(b), 8), cut] = value

        def add_rest(b, tile, value):
            offset = sz.main * sz.lanes + 128 * tile
            cut = (pl.ds(row_of(b), 8), slice(offset, offset + 128))
            pool[cut] = pool[cut] + value

        place_packed(sz, other, chunks[k], 3 * per, store_main, add_rest)
        start = sz.rest * other
        lanes = lane_iota(1)
        for c in range((sz.owners - 1) * sz.group):
            packed_rest = ghosts[k][pl.ds(4 * c + 3, 1), :]
            for i in range(3):
                place = pl.ds(i * sz.pool + sz.cells + c, 1)
                if sz.main:
                    cut = pl.ds(pl.multiple_of(other * sz.main, 128), 128)
                    pool[place, cut] = ghosts[k][pl.ds(4 * c + i, 1), :]
                value = pltpu.roll(packed_rest, lax.rem(start - i * sz.rest + 128, 128), 1)
                for tile in range(sz.rest_tiles):
                    offset = sz.main * sz.lanes + 128 * tile
                    inside = (lanes + 128 * tile >= start) & (
                        lanes + 128 * tile < start + sz.rest
                    )
                    cut = (place, slice(offset, offset + 128))
                    pool[cut] = pool[cut] + jnp.where(inside, value, 0.0)
    total = build_list(sz, me, lists, send, tasks)
    prepare(sz, lane, pool, bend, source_rows, centres, targets)
    all_tiles(sz, total, tasks, source_rows, centres, targets, offsets, sums, speeds, moved)
    for i in range(3):
        share_out[i] = share_rows(sz, pool, i * sz.pool, lane)
    for k in range(sz.lanes):
        blocks = [share_rows(sz, moved, i * sz.rows, lane ^ k) for i in range(3)]
        store_packed(sz, outs[k], blocks)


def share_rows(sz, ref, base, lane):
    if sz.share % 8 == 0:
        return ref[pl.ds(pl.multiple_of(base + lane * sz.share, 8), sz.share), :]
    rows = [ref[pl.ds(base + lane * sz.share + c, 1), :] for c in range(sz.share)]
    rows.append(jnp.zeros((8 - sz.share, rows[0].shape[1]), F32))
    return jnp.concatenate(rows, axis=0)


def last_kernel(sz, *refs):
    arrived, share, moved_out, velocity_out, held = (
        refs[: sz.lanes],
        refs[sz.lanes],
        refs[sz.lanes + 1],
        refs[sz.lanes + 2],
        refs[sz.lanes + 3],
    )
    lane = lax.axis_index("lane")
    held[...] = jnp.zeros_like(held)
    for k in range(sz.lanes):
        other = lane ^ k

        def store_main(b, m, value):
            held[b, :, pl.ds(pl.multiple_of(other * sz.main + 128 * m, 128), 128)] = value

        def add_rest(b, tile, value):
            offset = sz.main * sz.lanes + 128 * tile
            held[b, :, offset : offset + 128] = held[b, :, offset : offset + 128] + value

        place_packed(sz, other, arrived[k], 3, store_main, add_rest)
    for i in range(3):
        velocity = held[i]
        velocity_out[:, i, :] = velocity[: sz.share, : sz.points]
        moved_out[:, i, :] = (share[i] + TIME_STEP * velocity)[: sz.share, : sz.points]


def scratch(sz):
    return [
        pltpu.VMEM((3 * sz.pool, sz.width), F32),
        pltpu.VMEM((sz.tiles, SOURCE_ROWS * sz.pool, 128), F32),
        pltpu.VMEM((8 * sz.pool, 128), F32),
        pltpu.VMEM((sz.chunk_tiles, 8 * sz.rows, 128), F32),
        pltpu.VMEM((sz.chunk_tiles, 8 * sz.slots, 128), F32),
        pltpu.VMEM((sz.chunk_tiles, SUM_ROWS * sz.slots, 128), F32),
        pltpu.VMEM((3, sz.slots, sz.chunk_wide), F32),
        pltpu.VMEM((3 * sz.rows, sz.chunk_wide), F32),
        pltpu.SMEM((2, sz.slots), jnp.int32),
    ]


def swap(value, axis, size, k):
    return lax.ppermute(value, axis, [(d, d ^ k) for d in range(size)])


def shards(positions, bend_op, send_list, task_target, task_source, task_count):
    owners, lanes = lax.axis_size("space"), lax.axis_size("lane")
    cells, points = positions.shape[0], positions.shape[2]
    sz = sizes(owners, lanes, cells, points, task_target.shape[1], send_list.shape[1])
    params = pltpu.CompilerParams(vmem_limit_bytes=48 << 20)
    shape = jax.ShapeDtypeStruct
    cell = shape((sz.group, 3, points), F32)
    task_shape = shape((1, 2 * sz.cap + 1), jnp.int32)
    *leaving, own_list = pl.pallas_call(
        functools.partial(gather_kernel, sz),
        out_shape=[cell] * (owners - 1) + [task_shape],
        in_specs=[SMEM] * 4 + [ANY],
        out_specs=[ANY] * (owners - 1) + [SMEM],
        scratch_shapes=[pltpu.SemaphoreType.DMA((owners - 1, sz.group))],
        compiler_params=params,
        name="pick_cells",
    )(send_list, task_target, task_source, task_count, positions)
    ghosts = [swap(leaving[k - 1], "space", owners, k) for k in range(1, owners)]
    lists = [own_list] + [swap(own_list, "lane", lanes, k) for k in range(1, lanes)]
    wide = shape((pack_rows(sz, cells), 128), F32)
    narrow = shape((4 * sz.group, 128), F32)
    chunk, *leaving = pl.pallas_call(
        functools.partial(first_kernel, sz),
        out_shape=[wide] + [narrow] * (owners - 1),
        in_specs=[SMEM] * (1 + lanes) + [VMEM] * (1 + owners),
        out_specs=[VMEM] * owners,
        scratch_shapes=scratch(sz),
        compiler_params=params,
        name="first_step",
    )(send_list, *lists, positions, *ghosts, bend_op)
    arrived = [swap(leaving[k - 1], "space", owners, k) for k in range(1, owners)]
    chunks = [chunk] + [swap(chunk, "lane", lanes, k) for k in range(1, lanes)]
    arrived = jnp.concatenate(arrived, axis=0)
    ghosts = [arrived] + [swap(arrived, "lane", lanes, k) for k in range(1, lanes)]
    part = shape((pack_rows(sz, up(sz.share, 8)), 128), F32)
    share_shape = shape((3, up(sz.share, 8), sz.width), F32)
    *parts, share = pl.pallas_call(
        functools.partial(second_kernel, sz),
        out_shape=[part] * lanes + [share_shape],
        in_specs=[SMEM] * (1 + lanes) + [VMEM] * (2 * lanes + 1),
        out_specs=[VMEM] * (lanes + 1),
        scratch_shapes=scratch(sz),
        compiler_params=params,
        name="second_step",
    )(send_list, *lists, *chunks, *ghosts, bend_op)
    parts = [parts[0]] + [swap(parts[k], "lane", lanes, k) for k in range(1, lanes)]
    result = shape((sz.share, 3, points), F32)
    return pl.pallas_call(
        functools.partial(last_kernel, sz),
        out_shape=[result, result],
        in_specs=[VMEM] * (lanes + 1),
        out_specs=[VMEM] * 2,
        scratch_shapes=[pltpu.VMEM((3, up(sz.share, 8), sz.width), F32)],
        compiler_params=params,
        name="put_together",
    )(*parts, share)


def solution(mesh):
    in_specs = (
        P("space", None, None),
        P(),
        P("space", None),
        P(("space", "lane"), None),
        P(("space", "lane"), None),
        P(("space", "lane")),
    )
    out_specs = (P(("space", "lane"), None, None), P(("space", "lane"), None, None))
    return jax.shard_map(shards, mesh=mesh, in_specs=in_specs, out_specs=out_specs, check_vma=False)
```

time: 134 us -> 90.5 us (0.68); the launches traced: 133 us -> 92.2 us
  other arithmetic: 53.3 us -> 0 us
  blocking collectives: 42.4 us -> 0 us
  Pallas kernels: 0 us -> 32.9 us
  starting transfers between devices: 9.14 us -> 29.6 us
  waiting for transfers between devices: 4.93 us -> 22.6 us
  local copies, waits for them, and re-layouts: 16 us -> 5.76 us
  matrix products: 3.75 us -> 0 us
  loops' own time: 1.4 us -> 0 us
    reduce_sum x24 -> x0, other arithmetic: 51.1 us -> none  [stokes_tile(): jnp.sum(weight_direct * source_force[0][None, :] + weight_tensor * off_x,...]
    pallas_call x0 -> x4, Pallas kernels: none -> 32.9 us  [the longest x1 15.8 us: shards(): pl.pallas_call(functools.partial(second_kernel, sz), out_shape=[part] * l...]
    all_gather x2 -> x0, blocking collectives: 30.5 us -> none  [shards(): lax.all_gather(tiles, 'lane', axis=0, tiled=True)]
    ppermute x0 -> x26, starting transfers between devices: none -> 29.6 us  [swap(): return lax.ppermute(value, axis, [(d, d ^ k) for d in range(size)])]
    ppermute x0 -> x26, waiting for transfers between devices: none -> 22.6 us  [swap(): return lax.ppermute(value, axis, [(d, d ^ k) for d in range(size)])]
    unnamed x1 -> x0, blocking collectives: 11.9 us -> none
    all_to_all x2 -> x0, starting transfers between devices: 9.14 us -> none  [shards(): lax.all_to_all(outgoing, 'space', split_axis=0, concat_axis=0, tiled=True)]
    gather x8 -> x0, local copies, waits for them, and re-layouts: 5.94 us -> none  [the longest x2 2.25 us: tile_batch(): force_rows = pool_frc[slot_sources]]
  transfers between devices with their start and end apart: 2 -> 26, of which waited for: 1 -> 13; matrix products, arithmetic and copies ran while one was open for 1% -> 0% of each run, Pallas kernels for 0% -> 0%
where the time goes in v1:
time: 90.5 us; the launch traced here: 92.2 us
  Pallas kernels  32.9 us (36%)
  starting transfers between devices  29.6 us (33%)
  waiting for transfers between devices  22.6 us (25%)
  local copies, waits for them, and re-layouts  5.76 us (6%)
  between operations  1.37 us (2%)
    ppermute x26, starting transfers between devices, swap(): return lax.ppermute(value, axis, [(d, d ^ k) for d in range(size)])  29.6 us
    ppermute x26, waiting for transfers between devices, swap(): return lax.ppermute(value, axis, [(d, d ^ k) for d in range(size)])  22.6 us
    pallas_call x1, Pallas kernels, shards(): pl.pallas_call(functools.partial(second_kernel, sz), out_shape=[part] * l...  15.8 us
    pallas_call x1, Pallas kernels, shards(): pl.pallas_call(functools.partial(first_kernel, sz), out_shape=[wide] + [n...  15.6 us
    unnamed x13, local copies, waits for them, and re-layouts  4.43 us
  transfers between devices with their start and end apart: 26, of which 13 were waited for; matrix products, arithmetic and copies ran while one was open for 0% of the time, Pallas kernels for 0%

profile of v1, /device:TPU:0, one launch (start us, length us, event | category | flops | bytes accessed | tf_op | source)
XLA Modules:
  0.0 92.2 jit_solution(9955042905324606114)
XLA Ops:
  4.4 1.3 %pick_cells.1 = (f32[1,3,544]{2,1,0:T(4,128)S(1)}, f32[1,3,544]{2,1,0:T(4,128)S(1)}, f32[1,3,544]{2,1,0:T(4,128)S(1)}, f32[1,3,544]{2,1,0:T(4,128)S(1)}, f32[1,3...) custom-call(s32[1,8]{1,0:T(1,128)S(1)} %copy-done.2, ...), custom_call_target="tpu_custom_call" | custom-call | tf_op jit(solution)/shard_map/pick_cells/pallas_call | solution.py:461
  6.2 2.6 %collective-permute-start.4 = (f32[1,3,544]{2,1,0:T(4,128)S(1)}, f32[1,3,544]{2,1,0:T(4,128)S(1)}, u32[]{:S(2)}, u32[]{:S(2)}) collective-permute-start(f32[1,3,544]{2,1,0:T(4,128)S(1)} %get-tuple-element.25), channel_id=1, source_target_pairs={{0,8},{4,12},{8,0},{12,4},{16,24},{20,28},{24,16},{28,20},{1,9},{5... | collective-permute-start | bytes 19592 | tf_op jit(solution)/shard_map/ppermute | solution.py:450
  8.8 3.6 %collective-permute-start.2 = (s32[1,25]{1,0:T(1,128)S(1)}, s32[1,25]{1,0:T(1,128)S(1)}, u32[]{:S(2)}, u32[]{:S(2)}) collective-permute-start(s32[1,25]{1,0:T(1,128)S(1)} %get-tuple-element.23.refs_0_), channel_id=1, source_target_pairs={{0,3},{1,2},{2,1},{3,0},{4,7},{5,6},{6,5},{7,4},{8,11},{9,10},{10,... | collective-permute-start | bytes 308 | tf_op jit(solution)/shard_map/ppermute | solution.py:450
  14.1 2.7 %collective-permute-done.1.refs_2_ = s32[1,25]{1,0:T(1,128)S(1)} collective-permute-done((s32[1,25]{1,0:T(1,128)S(1)}, s32[1,25]{1,0:T(1,128)S(1)}, u32[]{:S(2)}, u32[]{:S(2)}) %collective-permute-start.1) | collective-permute-done | bytes 132 | tf_op jit(solution)/shard_map/ppermute | solution.py:450
  16.8 1.5 %collective-permute-start.6 = (f32[1,3,544]{2,1,0:T(4,128)S(1)}, f32[1,3,544]{2,1,0:T(4,128)S(1)}, u32[]{:S(2)}, u32[]{:S(2)}) collective-permute-start(f32[1,3,544]{2,1,0:T(4,128)S(1)} %get-tuple-element.27), channel_id=1, source_target_pairs={{0,16},{4,20},{8,24},{12,28},{16,0},{20,4},{24,8},{28,12},{1,17},{... | collective-permute-start | bytes 19592 | tf_op jit(solution)/shard_map/ppermute | solution.py:450
  18.9 2.3 %collective-permute-start.9 = (f32[1,3,544]{2,1,0:T(4,128)S(1)}, f32[1,3,544]{2,1,0:T(4,128)S(1)}, u32[]{:S(2)}, u32[]{:S(2)}) collective-permute-start(f32[1,3,544]{2,1,0:T(4,128)S(1)} %get-tuple-element.30), channel_id=1, source_target_pairs={{0,28},{4,24},{8,20},{12,16},{16,12},{20,8},{24,4},{28,0},{1,29},{... | collective-permute-start | bytes 19592 | tf_op jit(solution)/shard_map/ppermute | solution.py:450
  21.5 1.6 %collective-permute-done.8.refs_10_ = f32[1,3,544]{2,1,0:T(4,128)S(1)} collective-permute-done((f32[1,3,544]{2,1,0:T(4,128)S(1)}, f32[1,3,544]{2,1,0:T(4,128)S(1)}, u32[]{:S(2)}, u32[]{:S(2)}) %collective-permute-start.8) | collective-permute-done | bytes 6560 | tf_op jit(solution)/shard_map/ppermute | solution.py:450
  23.0 1.3 %copy-done = f32[544,544]{1,0:T(8,128)S(1)} copy-done((f32[544,544]{1,0:T(8,128)S(1)}, f32[544,544]{1,0:T(8,128)}, u32[]{:S(2)}) %copy-start) | copy-done | bytes 1183768
  24.4 15.6 %first_step.1 = (f32[104,128]{1,0:T(8,128)S(1)}, f32[4,128]{1,0:T(4,128)S(1)}, f32[4,128]{1,0:T(4,128)S(1)}, f32[4,128]{1,0:T(4,128)S(1)}, f32[4,128]{1,0:T(4,12...) custom-call(s32[1,8]{1,0:T(1,128)S(1)} %copy-done.2, ...), custom_call_target="tpu_custom_call" | custom-call | tf_op jit(solution)/shard_map/first_step/pallas_call | solution.py:474
  40.0 3.3 %collective-permute-start.12 = (f32[104,128]{1,0:T(8,128)S(1)}, f32[104,128]{1,0:T(8,128)S(1)}, u32[]{:S(2)}, u32[]{:S(2)}) collective-permute-start(f32[104,128]{1,0:T(8,128)S(1)} %get-tuple-element.31.refs_4_), channel_id=1, source_target_pairs={{0,3},{1,2},{2,1},{3,0},{4,7},{5,6},{6,5},{7,4},{8,11},{9,10},{10,... | collective-permute-start | bytes 159752 | tf_op jit(solution)/shard_map/ppermute | solution.py:450
  43.3 1.2 %collective-permute-start.10 = (f32[104,128]{1,0:T(8,128)S(1)}, f32[104,128]{1,0:T(8,128)S(1)}, u32[]{:S(2)}, u32[]{:S(2)}) collective-permute-start(f32[104,128]{1,0:T(8,128)S(1)} %get-tuple-element.31.refs_4_), channel_id=1, source_target_pairs={{0,1},{1,0},{2,3},{3,2},{4,5},{5,4},{6,7},{7,6},{8,9},{9,8},{10,11... | collective-permute-start | bytes 159752 | tf_op jit(solution)/shard_map/ppermute | solution.py:450
  44.4 1.9 %collective-permute-start.14 = (f32[4,128]{1,0:T(4,128)S(1)}, f32[4,128]{1,0:T(4,128)S(1)}, u32[]{:S(2)}, u32[]{:S(2)}) collective-permute-start(f32[4,128]{1,0:T(4,128)S(1)} %get-tuple-element.33), channel_id=1, source_target_pairs={{0,8},{4,12},{8,0},{12,4},{16,24},{20,28},{24,16},{28,20},{1,9},{5... | collective-permute-start | bytes 6152 | tf_op jit(solution)/shard_map/ppermute | solution.py:450
  48.0 1.4 %collective-permute-start.16 = (f32[4,128]{1,0:T(4,128)S(1)}, f32[4,128]{1,0:T(4,128)S(1)}, u32[]{:S(2)}, u32[]{:S(2)}) collective-permute-start(f32[4,128]{1,0:T(4,128)S(1)} %get-tuple-element.35), channel_id=1, source_target_pairs={{0,16},{4,20},{8,24},{12,28},{16,0},{20,4},{24,8},{28,12},{1,17},{... | collective-permute-start | bytes 6152 | tf_op jit(solution)/shard_map/ppermute | solution.py:450
  50.2 1.4 %collective-permute-done.16 = f32[4,128]{1,0:T(4,128)S(1)} collective-permute-done((f32[4,128]{1,0:T(4,128)S(1)}, f32[4,128]{1,0:T(4,128)S(1)}, u32[]{:S(2)}, u32[]{:S(2)}) %collective-permute-start.16) | collective-permute-done | bytes 2080 | tf_op jit(solution)/shard_map/ppermute | solution.py:450
  51.6 2.4 %collective-permute-start.18 = (f32[4,128]{1,0:T(4,128)S(1)}, f32[4,128]{1,0:T(4,128)S(1)}, u32[]{:S(2)}, u32[]{:S(2)}) collective-permute-start(f32[4,128]{1,0:T(4,128)S(1)} %get-tuple-element.37), channel_id=1, source_target_pairs={{0,24},{4,28},{8,16},{12,20},{16,8},{20,12},{24,0},{28,4},{1,25},{... | collective-permute-start | bytes 6152 | tf_op jit(solution)/shard_map/ppermute | solution.py:450
  54.1 2.0 %collective-permute-done.18 = f32[4,128]{1,0:T(4,128)S(1)} collective-permute-done((f32[4,128]{1,0:T(4,128)S(1)}, f32[4,128]{1,0:T(4,128)S(1)}, u32[]{:S(2)}, u32[]{:S(2)}) %collective-permute-start.18) | collective-permute-done | bytes 2080 | tf_op jit(solution)/shard_map/ppermute | solution.py:450
  56.1 1.8 %collective-permute-done.19 = f32[4,128]{1,0:T(4,128)S(1)} collective-permute-done((f32[4,128]{1,0:T(4,128)S(1)}, f32[4,128]{1,0:T(4,128)S(1)}, u32[]{:S(2)}, u32[]{:S(2)}) %collective-permute-start.19) | collective-permute-done | bytes 2080 | tf_op jit(solution)/shard_map/ppermute | solution.py:450
  58.0 1.5 %collective-permute-start.22 = (f32[28,128]{1,0:T(8,128)S(1)}, f32[28,128]{1,0:T(8,128)S(1)}, u32[]{:S(2)}, u32[]{:S(2)}) collective-permute-start(f32[28,128]{1,0:T(8,128)S(1)} %concatenate.3.refs_8_), channel_id=1, source_target_pairs={{0,3},{1,2},{2,1},{3,0},{4,7},{5,6},{6,5},{7,4},{8,11},{9,10},{10,... | collective-permute-start | bytes 43016 | tf_op jit(solution)/shard_map/ppermute | solution.py:450
  59.5 4.2 %collective-permute-done.22.refs_11_ = f32[28,128]{1,0:T(8,128)S(1)} collective-permute-done((f32[28,128]{1,0:T(8,128)S(1)}, f32[28,128]{1,0:T(8,128)S(1)}, u32[]{:S(2)}, u32[]{:S(2)}) %collective-permute-start.22) | collective-permute-done | bytes 14368 | tf_op jit(solution)/shard_map/ppermute | solution.py:450
  64.1 3.3 %collective-permute-done.20.refs_9_ = f32[28,128]{1,0:T(8,128)S(1)} collective-permute-done((f32[28,128]{1,0:T(8,128)S(1)}, f32[28,128]{1,0:T(8,128)S(1)}, u32[]{:S(2)}, u32[]{:S(2)}) %collective-permute-start.20) | collective-permute-done | bytes 14368 | tf_op jit(solution)/shard_map/ppermute | solution.py:450
  67.4 15.8 %second_step.1 = (f32[32,128]{1,0:T(8,128)S(1)}, f32[32,128]{1,0:T(8,128)S(1)}, f32[32,128]{1,0:T(8,128)S(1)}, f32[32,128]{1,0:T(8,128)S(1)}, f32[3,8,640]{2,1,0:T(8,128)S(1)}) custom-call(s32[1,8]{1,0:T(1,128)S(1)} %copy-done.3, s32[1,25]{1,0:T(1,128)S(1)} %get-tuple-element.23.refs_0_, s32[1,25]{1,0:T(1,128)S(1)} %collective-permute-done.refs_1_, ...), custom_call_target="tpu_custom_call" | custom-call | tf_op jit(solution)/shard_map/second_step/pallas_call | solution.py:489
  83.4 1.9 %collective-permute-start.24 = (f32[32,128]{1,0:T(8,128)S(1)}, f32[32,128]{1,0:T(8,128)S(1)}, u32[]{:S(2)}, u32[]{:S(2)}) collective-permute-start(f32[32,128]{1,0:T(8,128)S(1)} %get-tuple-element.41), channel_id=1, source_target_pairs={{0,2},{1,3},{2,0},{3,1},{4,6},{5,7},{6,4},{7,5},{8,10},{9,11},{10,... | collective-permute-start | bytes 49160 | tf_op jit(solution)/shard_map/ppermute | solution.py:450
  85.3 2.5 %collective-permute-start.25 = (f32[32,128]{1,0:T(8,128)S(1)}, f32[32,128]{1,0:T(8,128)S(1)}, u32[]{:S(2)}, u32[]{:S(2)}) collective-permute-start(f32[32,128]{1,0:T(8,128)S(1)} %get-tuple-element.42), channel_id=1, source_target_pairs={{0,3},{1,2},{2,1},{3,0},{4,7},{5,6},{6,5},{7,4},{8,11},{9,10},{10,... | collective-permute-start | bytes 49160 | tf_op jit(solution)/shard_map/ppermute | solution.py:450
  88.1 2.7 %collective-permute-done.25.refs_3_ = f32[32,128]{1,0:T(8,128)S(1)} collective-permute-done((f32[32,128]{1,0:T(8,128)S(1)}, f32[32,128]{1,0:T(8,128)S(1)}, u32[]{:S(2)}, u32[]{:S(2)}) %collective-permute-start.25) | collective-permute-done | bytes 16416 | tf_op jit(solution)/shard_map/ppermute | solution.py:450
  (48 shorter events, 11.1 us)
Async XLA Ops:
  5.7 12.7 %collective-permute-start.3 = (f32[1,3,544]{2,1,0:T(4,128)S(1)}, f32[1,3,544]{2,1,0:T(4,128)S(1)}, u32[]{:S(2)}, u32[]{:S(2)}) collective-permute-start(f32[1,3,544]{2,1,0:T(4,128)S(1)} %get-tuple-element.24), channel_id=1, source_target_pairs={{0,4},{4,0},{8,12},{12,8},{16,20},{20,16},{24,28},{28,24},{1,5},{5... | collective-permute-start | bytes 19592 | tf_op jit(solution)/shard_map/ppermute | solution.py:450
  6.2 12.7 %collective-permute-start.4 = (f32[1,3,544]{2,1,0:T(4,128)S(1)}, f32[1,3,544]{2,1,0:T(4,128)S(1)}, u32[]{:S(2)}, u32[]{:S(2)}) collective-permute-start(f32[1,3,544]{2,1,0:T(4,128)S(1)} %get-tuple-element.25), channel_id=1, source_target_pairs={{0,8},{4,12},{8,0},{12,4},{16,24},{20,28},{24,16},{28,20},{1,9},{5... | collective-permute-start | bytes 19592 | tf_op jit(solution)/shard_map/ppermute | solution.py:450
  8.8 5.3 %collective-permute-start.2 = (s32[1,25]{1,0:T(1,128)S(1)}, s32[1,25]{1,0:T(1,128)S(1)}, u32[]{:S(2)}, u32[]{:S(2)}) collective-permute-start(s32[1,25]{1,0:T(1,128)S(1)} %get-tuple-element.23.refs_0_), channel_id=1, source_target_pairs={{0,3},{1,2},{2,1},{3,0},{4,7},{5,6},{6,5},{7,4},{8,11},{9,10},{10,... | collective-permute-start | bytes 308 | tf_op jit(solution)/shard_map/ppermute | solution.py:450
  12.4 4.4 %collective-permute-start.1 = (s32[1,25]{1,0:T(1,128)S(1)}, s32[1,25]{1,0:T(1,128)S(1)}, u32[]{:S(2)}, u32[]{:S(2)}) collective-permute-start(s32[1,25]{1,0:T(1,128)S(1)} %get-tuple-element.23.refs_0_), channel_id=1, source_target_pairs={{0,2},{1,3},{2,0},{3,1},{4,6},{5,7},{6,4},{7,5},{8,10},{9,11},{10,... | collective-permute-start | bytes 308 | tf_op jit(solution)/shard_map/ppermute | solution.py:450
  12.4 6.0 %collective-permute-start = (s32[1,25]{1,0:T(1,128)S(1)}, s32[1,25]{1,0:T(1,128)S(1)}, u32[]{:S(2)}, u32[]{:S(2)}) collective-permute-start(s32[1,25]{1,0:T(1,128)S(1)} %get-tuple-element.23.refs_0_), channel_id=1, source_target_pairs={{0,1},{1,0},{2,3},{3,2},{4,5},{5,4},{6,7},{7,6},{8,9},{9,8},{10,11... | collective-permute-start | bytes 308 | tf_op jit(solution)/shard_map/ppermute | solution.py:450
  14.1 7.1 %collective-permute-start.5 = (f32[1,3,544]{2,1,0:T(4,128)S(1)}, f32[1,3,544]{2,1,0:T(4,128)S(1)}, u32[]{:S(2)}, u32[]{:S(2)}) collective-permute-start(f32[1,3,544]{2,1,0:T(4,128)S(1)} %get-tuple-element.26), channel_id=1, source_target_pairs={{0,12},{4,8},{8,4},{12,0},{16,28},{20,24},{24,20},{28,16},{1,13},{... | collective-permute-start | bytes 19592 | tf_op jit(solution)/shard_map/ppermute | solution.py:450
  16.8 4.4 %collective-permute-start.6 = (f32[1,3,544]{2,1,0:T(4,128)S(1)}, f32[1,3,544]{2,1,0:T(4,128)S(1)}, u32[]{:S(2)}, u32[]{:S(2)}) collective-permute-start(f32[1,3,544]{2,1,0:T(4,128)S(1)} %get-tuple-element.27), channel_id=1, source_target_pairs={{0,16},{4,20},{8,24},{12,28},{16,0},{20,4},{24,8},{28,12},{1,17},{... | collective-permute-start | bytes 19592 | tf_op jit(solution)/shard_map/ppermute | solution.py:450
  18.4 4.7 %collective-permute-start.8 = (f32[1,3,544]{2,1,0:T(4,128)S(1)}, f32[1,3,544]{2,1,0:T(4,128)S(1)}, u32[]{:S(2)}, u32[]{:S(2)}) collective-permute-start(f32[1,3,544]{2,1,0:T(4,128)S(1)} %get-tuple-element.29), channel_id=1, source_target_pairs={{0,24},{4,28},{8,16},{12,20},{16,8},{20,12},{24,0},{28,4},{1,25},{... | collective-permute-start | bytes 19592 | tf_op jit(solution)/shard_map/ppermute | solution.py:450
  18.9 4.1 %collective-permute-start.9 = (f32[1,3,544]{2,1,0:T(4,128)S(1)}, f32[1,3,544]{2,1,0:T(4,128)S(1)}, u32[]{:S(2)}, u32[]{:S(2)}) collective-permute-start(f32[1,3,544]{2,1,0:T(4,128)S(1)} %get-tuple-element.30), channel_id=1, source_target_pairs={{0,28},{4,24},{8,20},{12,16},{16,12},{20,8},{24,4},{28,0},{1,29},{... | collective-permute-start | bytes 19592 | tf_op jit(solution)/shard_map/ppermute | solution.py:450
  40.0 27.4 %collective-permute-start.12 = (f32[104,128]{1,0:T(8,128)S(1)}, f32[104,128]{1,0:T(8,128)S(1)}, u32[]{:S(2)}, u32[]{:S(2)}) collective-permute-start(f32[104,128]{1,0:T(8,128)S(1)} %get-tuple-element.31.refs_4_), channel_id=1, source_target_pairs={{0,3},{1,2},{2,1},{3,0},{4,7},{5,6},{6,5},{7,4},{8,11},{9,10},{10,... | collective-permute-start | bytes 159752 | tf_op jit(solution)/shard_map/ppermute | solution.py:450
  43.3 24.1 %collective-permute-start.11 = (f32[104,128]{1,0:T(8,128)S(1)}, f32[104,128]{1,0:T(8,128)S(1)}, u32[]{:S(2)}, u32[]{:S(2)}) collective-permute-start(f32[104,128]{1,0:T(8,128)S(1)} %get-tuple-element.31.refs_4_), channel_id=1, source_target_pairs={{0,2},{1,3},{2,0},{3,1},{4,6},{5,7},{6,4},{7,5},{8,10},{9,11},{10,... | collective-permute-start | bytes 159752 | tf_op jit(solution)/shard_map/ppermute | solution.py:450
  43.3 24.1 %collective-permute-start.10 = (f32[104,128]{1,0:T(8,128)S(1)}, f32[104,128]{1,0:T(8,128)S(1)}, u32[]{:S(2)}, u32[]{:S(2)}) collective-permute-start(f32[104,128]{1,0:T(8,128)S(1)} %get-tuple-element.31.refs_4_), channel_id=1, source_target_pairs={{0,1},{1,0},{2,3},{3,2},{4,5},{5,4},{6,7},{7,6},{8,9},{9,8},{10,11... | collective-permute-start | bytes 159752 | tf_op jit(solution)/shard_map/ppermute | solution.py:450
  44.4 3.6 %collective-permute-start.14 = (f32[4,128]{1,0:T(4,128)S(1)}, f32[4,128]{1,0:T(4,128)S(1)}, u32[]{:S(2)}, u32[]{:S(2)}) collective-permute-start(f32[4,128]{1,0:T(4,128)S(1)} %get-tuple-element.33), channel_id=1, source_target_pairs={{0,8},{4,12},{8,0},{12,4},{16,24},{20,28},{24,16},{28,20},{1,9},{5... | collective-permute-start | bytes 6152 | tf_op jit(solution)/shard_map/ppermute | solution.py:450
  46.3 3.2 %collective-permute-start.15 = (f32[4,128]{1,0:T(4,128)S(1)}, f32[4,128]{1,0:T(4,128)S(1)}, u32[]{:S(2)}, u32[]{:S(2)}) collective-permute-start(f32[4,128]{1,0:T(4,128)S(1)} %get-tuple-element.34), channel_id=1, source_target_pairs={{0,12},{4,8},{8,4},{12,0},{16,28},{20,24},{24,20},{28,16},{1,13},{... | collective-permute-start | bytes 6152 | tf_op jit(solution)/shard_map/ppermute | solution.py:450
  48.0 3.6 %collective-permute-start.16 = (f32[4,128]{1,0:T(4,128)S(1)}, f32[4,128]{1,0:T(4,128)S(1)}, u32[]{:S(2)}, u32[]{:S(2)}) collective-permute-start(f32[4,128]{1,0:T(4,128)S(1)} %get-tuple-element.35), channel_id=1, source_target_pairs={{0,16},{4,20},{8,24},{12,28},{16,0},{20,4},{24,8},{28,12},{1,17},{... | collective-permute-start | bytes 6152 | tf_op jit(solution)/shard_map/ppermute | solution.py:450
  49.5 4.5 %collective-permute-start.17 = (f32[4,128]{1,0:T(4,128)S(1)}, f32[4,128]{1,0:T(4,128)S(1)}, u32[]{:S(2)}, u32[]{:S(2)}) collective-permute-start(f32[4,128]{1,0:T(4,128)S(1)} %get-tuple-element.36), channel_id=1, source_target_pairs={{0,20},{4,16},{8,28},{12,24},{16,4},{20,0},{24,12},{28,8},{1,21},{... | collective-permute-start | bytes 6152 | tf_op jit(solution)/shard_map/ppermute | solution.py:450
  51.6 4.5 %collective-permute-start.18 = (f32[4,128]{1,0:T(4,128)S(1)}, f32[4,128]{1,0:T(4,128)S(1)}, u32[]{:S(2)}, u32[]{:S(2)}) collective-permute-start(f32[4,128]{1,0:T(4,128)S(1)} %get-tuple-element.37), channel_id=1, source_target_pairs={{0,24},{4,28},{8,16},{12,20},{16,8},{20,12},{24,0},{28,4},{1,25},{... | collective-permute-start | bytes 6152 | tf_op jit(solution)/shard_map/ppermute | solution.py:450
  54.0 3.9 %collective-permute-start.19 = (f32[4,128]{1,0:T(4,128)S(1)}, f32[4,128]{1,0:T(4,128)S(1)}, u32[]{:S(2)}, u32[]{:S(2)}) collective-permute-start(f32[4,128]{1,0:T(4,128)S(1)} %get-tuple-element.38), channel_id=1, source_target_pairs={{0,28},{4,24},{8,20},{12,16},{16,12},{20,8},{24,4},{28,0},{1,29},{... | collective-permute-start | bytes 6152 | tf_op jit(solution)/shard_map/ppermute | solution.py:450
  58.0 5.7 %collective-permute-start.22 = (f32[28,128]{1,0:T(8,128)S(1)}, f32[28,128]{1,0:T(8,128)S(1)}, u32[]{:S(2)}, u32[]{:S(2)}) collective-permute-start(f32[28,128]{1,0:T(8,128)S(1)} %concatenate.3.refs_8_), channel_id=1, source_target_pairs={{0,3},{1,2},{2,1},{3,0},{4,7},{5,6},{6,5},{7,4},{8,11},{9,10},{10,... | collective-permute-start | bytes 43016 | tf_op jit(solution)/shard_map/ppermute | solution.py:450
  59.5 4.6 %collective-permute-start.21 = (f32[28,128]{1,0:T(8,128)S(1)}, f32[28,128]{1,0:T(8,128)S(1)}, u32[]{:S(2)}, u32[]{:S(2)}) collective-permute-start(f32[28,128]{1,0:T(8,128)S(1)} %concatenate.3.refs_8_), channel_id=1, source_target_pairs={{0,2},{1,3},{2,0},{3,1},{4,6},{5,7},{6,4},{7,5},{8,10},{9,11},{10,... | collective-permute-start | bytes 43016 | tf_op jit(solution)/shard_map/ppermute | solution.py:450
  63.7 3.7 %collective-permute-start.20 = (f32[28,128]{1,0:T(8,128)S(1)}, f32[28,128]{1,0:T(8,128)S(1)}, u32[]{:S(2)}, u32[]{:S(2)}) collective-permute-start(f32[28,128]{1,0:T(8,128)S(1)} %concatenate.3.refs_8_), channel_id=1, source_target_pairs={{0,1},{1,0},{2,3},{3,2},{4,5},{5,4},{6,7},{7,6},{8,9},{9,8},{10,11... | collective-permute-start | bytes 43016 | tf_op jit(solution)/shard_map/ppermute | solution.py:450
  83.3 4.5 %collective-permute-start.23 = (f32[32,128]{1,0:T(8,128)S(1)}, f32[32,128]{1,0:T(8,128)S(1)}, u32[]{:S(2)}, u32[]{:S(2)}) collective-permute-start(f32[32,128]{1,0:T(8,128)S(1)} %get-tuple-element.40), channel_id=1, source_target_pairs={{0,1},{1,0},{2,3},{3,2},{4,5},{5,4},{6,7},{7,6},{8,9},{9,8},{10,11... | collective-permute-start | bytes 49160 | tf_op jit(solution)/shard_map/ppermute | solution.py:450
  83.4 4.7 %collective-permute-start.24 = (f32[32,128]{1,0:T(8,128)S(1)}, f32[32,128]{1,0:T(8,128)S(1)}, u32[]{:S(2)}, u32[]{:S(2)}) collective-permute-start(f32[32,128]{1,0:T(8,128)S(1)} %get-tuple-element.41), channel_id=1, source_target_pairs={{0,2},{1,3},{2,0},{3,1},{4,6},{5,7},{6,4},{7,5},{8,10},{9,11},{10,... | collective-permute-start | bytes 49160 | tf_op jit(solution)/shard_map/ppermute | solution.py:450
  85.3 5.5 %collective-permute-start.25 = (f32[32,128]{1,0:T(8,128)S(1)}, f32[32,128]{1,0:T(8,128)S(1)}, u32[]{:S(2)}, u32[]{:S(2)}) collective-permute-start(f32[32,128]{1,0:T(8,128)S(1)} %get-tuple-element.42), channel_id=1, source_target_pairs={{0,3},{1,2},{2,1},{3,0},{4,7},{5,6},{6,5},{7,4},{8,11},{9,10},{10,... | collective-permute-start | bytes 49160 | tf_op jit(solution)/shard_map/ppermute | solution.py:450
  (8 other events, 118.1 us)
